TPU v7x, 512 devices: a whole 4x8x8 slice. The times are simulated.
512 devices in a mesh: dp: 8 (over y), feat: 64 (over x, z, core).
Axes of the slice: x: 4, y: 8, z: 8, core: 2. Of those that a mesh axis runs over, the one named last changes fastest.
Arguments:
- features: bfloat16 [8, 16384, 128], P('dp', None, 'feat'), may hold values from -6 to 6
- tile_weights: bfloat16 [8, 1536, 128, 128], P('dp', 'feat'), may hold values from -0.15625 to 0.15625
- tile_rows: int32 [8, 1536], P('dp', 'feat'), may hold values from 0 to 1
- tile_owners: int32 [8, 1536, 1], P('dp', 'feat'), may hold values from 0 to 63; in each aligned block of 24 rows (0 to 23, 24 to 47, ..., all dimensions but the last counted through in order) at most 2 rows name the same one
- tile_blocks: int32 [8, 1536], P('dp', 'feat'), may hold values from 0 to 1
- tile_counts: int32 [8, 64], P('dp', 'feat'), may hold values from 6 to 24, as said below
- cotangent: bfloat16 [8, 16384, 1024], P('dp', 'feat'), may hold values from -0.046875 to 0.046875
- w_self: bfloat16 [128, 1024], replicated, may hold values from -0.5 to 0.5
- w_neigh: bfloat16 [128, 1024], replicated, may hold values from -0.5 to 0.5
- bias: float32 [1024], replicated, may hold values from -4 to 4
Outputs:
- grad_self: float32 [128, 1024], P(None, 'feat')
- grad_neigh: float32 [128, 1024], P(None, 'feat')
- grad_bias: float32 [1024], P('feat')
Inputs may be any that keep to these rules, and one draw needn't show every extreme that they name: `tile_owners`: among the 24 tile slots of one device at most 2 name one owner, a bound that some block of them reaches. `tile_counts`: in every batch some device has all 24 slots live.
All inputs are finite; a program needn't handle non-finite values.
Results may differ from a plain program's by a relative error of at most 0.008.
Values may be sent and summed in bfloat16 or wider, within the bound.
No kernel may reach another device: no remote copies, remote signals or barrier semaphores. Data moves between devices by JAX's collectives and lax.ppermute only.
A program may use at most 64 MiB of HBM per device.

v0:
```python
import jax
import jax.numpy as jnp
from jax import lax
from jax.sharding import PartitionSpec as P


def silu_slope(pre_act):
    sigmoid_z = jax.nn.sigmoid(pre_act)
    return sigmoid_z * (1.0 + pre_act * (1.0 - sigmoid_z))


def local(
    features,
    tile_weights,
    tile_rows,
    tile_owners,
    tile_blocks,
    tile_counts,
    cotangent,
    w_self,
    w_neigh,
    bias,
):
    owned = lax.all_to_all(features, "feat", split_axis=1, concat_axis=2, tiled=True)[0]
    node_rows, feat_width = owned.shape
    slot_count = tile_weights.shape[1]
    tile_side = tile_weights.shape[2]
    row_blocks = node_rows // tile_side
    peer_count = lax.axis_size("feat")
    row_index = tile_rows[0]
    owner_index = tile_owners[0, :, 0]
    block_index = tile_blocks[0]
    live = jnp.arange(slot_count, dtype=jnp.int32) < tile_counts[0, 0]
    whole = lax.all_gather(owned, "feat", axis=0, tiled=True)
    picked = whole.reshape(-1, tile_side, feat_width)[owner_index * row_blocks + block_index]
    products = jnp.einsum(
        "kij,kjf->kif", tile_weights[0], picked, preferred_element_type=jnp.float32
    )
    select = (
        (row_index[None, :] == jnp.arange(row_blocks, dtype=jnp.int32)[:, None]) & live[None, :]
    ).astype(jnp.float32)
    summed = jnp.einsum("rk,kif->rif", select, products, precision=lax.Precision.HIGHEST)
    neighbour = summed.reshape(node_rows, feat_width).astype(jnp.bfloat16)
    pre_act = (
        jnp.dot(owned, w_self, preferred_element_type=jnp.float32)
        + jnp.dot(neighbour, w_neigh, preferred_element_type=jnp.float32)
        + bias
    )
    slope = (cotangent[0].astype(jnp.float32) * silu_slope(pre_act)).astype(jnp.bfloat16)
    grad_s = jnp.einsum("nf,nh->fh", owned, slope, preferred_element_type=jnp.float32)
    grad_n = jnp.einsum("nf,nh->fh", neighbour, slope, preferred_element_type=jnp.float32)
    grad_b = jnp.sum(slope.astype(jnp.float32), axis=0)
    total_s, total_n, total_b = lax.psum((grad_s, grad_n, grad_b), ("dp", "feat"))
    column_count = w_self.shape[1] // peer_count
    start = lax.axis_index("feat") * column_count
    out_s = lax.dynamic_slice_in_dim(total_s, start, column_count, 1)
    out_n = lax.dynamic_slice_in_dim(total_n, start, column_count, 1)
    out_b = lax.dynamic_slice_in_dim(total_b, start, column_count, 0)
    return (out_s, out_n, out_b)


def solution(mesh):
    return jax.shard_map(
        local,
        mesh=mesh,
        in_specs=(
            P("dp", None, "feat"),
            P("dp", "feat", None, None),
            P("dp", "feat"),
            P("dp", "feat", None),
            P("dp", "feat"),
            P("dp", "feat"),
            P("dp", "feat", None),
            P(),
            P(),
            P(),
        ),
        out_specs=(P(None, "feat"), P(None, "feat"), P("feat")),
        check_vma=False,
    )
```

profile of v0, /device:TPU:23, one launch (start us, length us, event | category | flops | bytes accessed | tf_op | source)
XLA Modules:
  0.0 554.2 jit_solution(6314317441695136422)
XLA Ops:
  7.2 15.4 %copy.26 = bf16[1,16384,2]{2,0,1:T(2,128)(2,1)} copy(bf16[1,16384,2]{1,2,0:T(2,128)(2,1)} %param.10) | data formatting | bytes 131072 | tf_op args[0]
  22.6 0.5 broadcast.52
  23.1 90.8 %reduce = bf16[16384,2]{1,0:T(8,128)(2,1)} reduce(bf16[16384,1,2]{2,1,0:T(2,128)(2,1)} %bitcast.51, bf16[]{:T(256)} %broadcast.52), dimensions={1}, to_apply=%bitcast.36.reduce_sub_computation | reduce | bytes 131074
  113.9 7.1 %reshape.61 = bf16[64,2,256]{2,1,0:T(2,128)(2,1)S(1)} reshape(bf16[16384,2]{1,0:T(8,128)(2,1)} %reduce) | data formatting | bytes 131072
  121.0 21.9 %all_to_all.15 = bf16[64,2,256]{2,1,0:T(2,128)(2,1)S(1)} all-to-all(bf16[64,2,256]{2,1,0:T(2,128)(2,1)S(1)} %reshape.61), channel_id=1, replica_groups=mesh['dp'=8,'feat'=64] {'feat'}, dimensions={0} | all-to-all | bytes 131072 | tf_op jit(solution)/shard_map/all_to_all | solution.py:24
  142.9 16.4 %reshape.62 = bf16[16384,1,2]{2,1,0:T(2,128)(2,1)} reshape(bf16[64,2,256]{2,1,0:T(2,128)(2,1)S(1)} %all_to_all.15) | data formatting | bytes 131072
  159.3 15.4 %copy.27 = bf16[1,16384,2]{1,2,0:T(2,128)(2,1)S(1)} copy(bf16[1,16384,2]{2,0,1:T(2,128)(2,1)} %bitcast.52) | data formatting | bytes 131072 | tf_op jit(solution)/shard_map/all_to_all | solution.py:24
  174.7 0.1 copy.28
  174.8 0.7 squeeze.14
  175.5 0.2 all-reduce.3.cloned.1.call-start
  176.4 1.2 fusion.10
  177.6 77.5 %all-gather.2.cloned.1.call-done = bf16[16384,128]{0,1:T(8,128)(2,1)} async-done(((bf16[256,128]{0,1:T(8,128)(2,1)}), bf16[16384,128]{0,1:T(8,128)(2,1)}) %all-gather.2.cloned.1.call-update) | async-done | bytes 4194320 | tf_op jit(solution)/shard_map/all_gather | solution.py:34
  255.0 6.4 %copy.29 = bf16[16384,128]{1,0:T(8,128)(2,1)} copy(bf16[16384,128]{0,1:T(8,128)(2,1)} %all-gather.2.cloned.1.call-done) | data formatting | bytes 8388608 | tf_op jit(solution)/shard_map/all_gather | solution.py:34
  261.4 2.9 gather_fusion
  264.4 1.9 convolution_bitcast_fusion
  266.2 2.0 copy.31
  268.2 0.6 convolution_convert_fusion
  268.9 1.8 convert_reduce_fusion
  270.6 1.1 fusion.11
  271.8 1.1 convolution_bitcast_fusion.1
  272.9 96.3 %psum.23 = f32[1024]{0:T(1024)S(1)} all-reduce(f32[1024]{0:T(1024)S(1)} %get-tuple-element.5), channel_id=1, replica_groups=mesh['dp'=8,'feat'=64] {'dp','feat'}, use_global_device_ids=true, to_apply=%region_3.0 | all-reduce | flops 1024 | bytes 8192 | tf_op jit(solution)/shard_map/psum | solution.py:53
  369.3 0.6 dynamic_slice.11
  369.9 176.2 %all-reduce.3.cloned.1.call-done = (f32[128,1024]{0,1:T(8,128)}, f32[128,1024]{0,1:T(8,128)}) async-done(((f32[128,1024]{0,1:T(8,128)}, f32[128,1024]{0,1:T(8,128)}), (f32[128,1024]{0,1:T(8,128)}, f32[128,1024]{0,1:T(8,128)})) %all-reduce.3.cloned.1.call-update) | async-done | bytes 1048592 | tf_op jit(solution)/shard_map/psum | solution.py:53
  546.0 1.3 constant_dynamic-slice_fusion
  (22 shorter events, 0.1 us)
Async XLA Ops:
  7.2 257.2 %copy-start = (bf16[1,24,128,128]{3,2,1,0:T(8,128)(2,1)S(1)}, bf16[1,24,128,128]{3,2,1,0:T(8,128)(2,1)}, u32[]{:S(2)}) copy-start(bf16[1,24,128,128]{3,2,1,0:T(8,128)(2,1)} %param.11) | copy-start | bytes 2359300
  7.2 247.8 %all-gather.2.cloned.1.call-start = ((), (), s32[]{:S(2)}) async-start(), calls=%async_computation.1 | async-start | bytes 4259840 | tf_op jit(solution)/shard_map/all_gather | solution.py:34
  159.3 17.1 %copy-start.5 = (s32[1,24]{1,0:T(1,128)S(1)}, s32[1,24]{1,0:T(1,128)}, u32[]{:S(2)}) copy-start(s32[1,24]{1,0:T(1,128)} %param.14) | copy-start | bytes 292
  159.3 17.1 %copy-start.6 = (s32[1,24,1]{1,2,0:T(1,128)S(1)}, s32[1,24,1]{1,2,0:T(1,128)}, u32[]{:S(2)}) copy-start(s32[1,24,1]{1,2,0:T(1,128)} %param.13) | copy-start | bytes 292
  159.3 17.1 %copy-start.2 = (bf16[128,1024]{1,0:T(8,128)(2,1)S(1)}, bf16[128,1024]{1,0:T(8,128)(2,1)}, u32[]{:S(2)}) copy-start(bf16[128,1024]{1,0:T(8,128)(2,1)} %param.17) | copy-start | bytes 786436
  175.5 370.6 %all-reduce.3.cloned.1.call-start = ((), (), s32[]{:S(2)}) async-start(), calls=%async_computation.2 | async-start | bytes 2097152 | tf_op jit(solution)/shard_map/psum | solution.py:53
  261.4 6.8 %copy-start.3 = (s32[1,24]{1,0:T(1,128)S(1)}, s32[1,24]{1,0:T(1,128)}, u32[]{:S(2)}) copy-start(s32[1,24]{1,0:T(1,128)} %param.12) | copy-start | bytes 292
  264.4 4.5 copy-start.4
  268.8 3.0 copy-start.1
Sparse Core Ops, SparseCore 0:
  175.6 79.3 all-gather.1
  273.1 272.9 all-reduce.2
where the time goes:
time: 556 us; the launch traced here: 554 us
  waiting for transfers between devices  254 us (46%)
  blocking collectives  118 us (21%)
  other arithmetic  90.8 us (16%)
  local copies, waits for them, and re-layouts  68.7 us (12%)
  between operations  14.9 us (3%)
  matrix products  7.67 us (1%)
    psum x1, waiting for transfers between devices, local(): lax.psum((grad_s, grad_n, grad_b), ('dp', 'feat'))  176 us
    psum x1, blocking collectives, local(): lax.psum((grad_s, grad_n, grad_b), ('dp', 'feat'))  96.3 us
    unnamed x1, other arithmetic  90.8 us
    all_gather x1, waiting for transfers between devices, local(): whole = lax.all_gather(owned, 'feat', axis=0, tiled=True)  77.5 us
    unnamed x19, local copies, waits for them, and re-layouts  39.5 us
    all_to_all x1, blocking collectives, local(): lax.all_to_all(features, 'feat', split_axis=1, concat_axis=2, tiled=True)[0]  21.9 us
    all_to_all x2, local copies, waits for them, and re-layouts, local(): lax.all_to_all(features, 'feat', split_axis=1, concat_axis=2, tiled=True)[0]  15.5 us
  transfers between devices with their start and end apart: 2, of which 2 were waited for; matrix products, arithmetic and copies ran while one was open for 0% of the time, Pallas kernels for 0%

commit v1 on v0

--- a/solution.py
+++ b/solution.py
@@ -1,7 +1,18 @@
+import functools
 import jax
 import jax.numpy as jnp
 from jax import lax
 from jax.sharding import PartitionSpec as P
+from jax.lax import psum
+
+
+def state_circles_in(chunk, mesh_ax, axis_key):
+    for it in (mesh_ax, axis_key):
+        chunk = psum(chunk, it)
+    return chunk
+
+
+paths_guide = functools.partial(state_circles_in, mesh_ax="dp", axis_key="feat")
 
 
 def silu_slope(pre_act):
@@ -50,7 +61,7 @@
     grad_s = jnp.einsum("nf,nh->fh", owned, slope, preferred_element_type=jnp.float32)
     grad_n = jnp.einsum("nf,nh->fh", neighbour, slope, preferred_element_type=jnp.float32)
     grad_b = jnp.sum(slope.astype(jnp.float32), axis=0)
-    total_s, total_n, total_b = lax.psum((grad_s, grad_n, grad_b), ("dp", "feat"))
+    total_s, total_n, total_b = paths_guide((grad_s, grad_n, grad_b))
     column_count = w_self.shape[1] // peer_count
     start = lax.axis_index("feat") * column_count
     out_s = lax.dynamic_slice_in_dim(total_s, start, column_count, 1)

time: 556 us -> 562 us (1.011)
  the two profiles are of different devices: /device:TPU:23 before, /device:TPU:8 now
where the time goes in v1:
time: 562 us; the launch traced here: 561 us
  waiting for transfers between devices  216 us (38%)
  blocking collectives  163 us (29%)
  other arithmetic  90.8 us (16%)
  local copies, waits for them, and re-layouts  68.9 us (12%)
  between operations  14.6 us (3%)
  matrix products  7.7 us (1%)
    psum x2, waiting for transfers between devices, state_circles_in(): chunk = psum(chunk, it)  140 us
    psum x2, blocking collectives, state_circles_in(): chunk = psum(chunk, it)  140 us
    unnamed x1, other arithmetic  90.7 us
    all_gather x1, waiting for transfers between devices, local(): whole = lax.all_gather(owned, 'feat', axis=0, tiled=True)  75.8 us
    unnamed x19, local copies, waits for them, and re-layouts  39.6 us
    all_to_all x1, blocking collectives, local(): lax.all_to_all(features, 'feat', split_axis=1, concat_axis=2, tiled=True)[0]  23.3 us
    all_to_all x2, local copies, waits for them, and re-layouts, local(): lax.all_to_all(features, 'feat', split_axis=1, concat_axis=2, tiled=True)[0]  15.5 us
  transfers between devices with their start and end apart: 3, of which 3 were waited for; matrix products, arithmetic and copies ran while one was open for 0% of the time, Pallas kernels for 0%

profile of v1, /device:TPU:8, one launch (start us, length us, event | category | flops | bytes accessed | tf_op | source)
XLA Modules:
  0.0 561.0 jit_solution(4517570862706635124)
XLA Ops:
  7.2 15.4 %copy.26 = bf16[1,16384,2]{2,0,1:T(2,128)(2,1)} copy(bf16[1,16384,2]{1,2,0:T(2,128)(2,1)} %param.10) | data formatting | bytes 131072 | tf_op args[0]
  22.6 0.5 broadcast.52
  23.1 90.7 %reduce = bf16[16384,2]{1,0:T(8,128)(2,1)} reduce(bf16[16384,1,2]{2,1,0:T(2,128)(2,1)} %bitcast.51, bf16[]{:T(256)} %broadcast.52), dimensions={1}, to_apply=%bitcast.36.reduce_sub_computation | reduce | bytes 131074
  113.9 7.1 %reshape.61 = bf16[64,2,256]{2,1,0:T(2,128)(2,1)S(1)} reshape(bf16[16384,2]{1,0:T(8,128)(2,1)} %reduce) | data formatting | bytes 131072
  121.0 23.3 %all_to_all.15 = bf16[64,2,256]{2,1,0:T(2,128)(2,1)S(1)} all-to-all(bf16[64,2,256]{2,1,0:T(2,128)(2,1)S(1)} %reshape.61), channel_id=1, replica_groups=mesh['dp'=8,'feat'=64] {'feat'}, dimensions={0} | all-to-all | bytes 131072 | tf_op jit(solution)/shard_map/all_to_all | solution.py:35
  144.3 16.5 %reshape.62 = bf16[16384,1,2]{2,1,0:T(2,128)(2,1)} reshape(bf16[64,2,256]{2,1,0:T(2,128)(2,1)S(1)} %all_to_all.15) | data formatting | bytes 131072
  160.8 15.4 %copy.27 = bf16[1,16384,2]{1,2,0:T(2,128)(2,1)S(1)} copy(bf16[1,16384,2]{2,0,1:T(2,128)(2,1)} %bitcast.52) | data formatting | bytes 131072 | tf_op jit(solution)/shard_map/all_to_all | solution.py:35
  176.3 0.7 squeeze.14
  178.0 1.2 fusion.10
  179.1 75.8 %all-gather.2.cloned.1.call-done = bf16[16384,128]{0,1:T(8,128)(2,1)} async-done(((bf16[256,128]{0,1:T(8,128)(2,1)}), bf16[16384,128]{0,1:T(8,128)(2,1)}) %all-gather.2.cloned.1.call-update) | async-done | bytes 4194320 | tf_op jit(solution)/shard_map/all_gather | solution.py:45
  254.9 6.4 %copy.29 = bf16[16384,128]{1,0:T(8,128)(2,1)} copy(bf16[16384,128]{0,1:T(8,128)(2,1)} %all-gather.2.cloned.1.call-done) | data formatting | bytes 8388608 | tf_op jit(solution)/shard_map/all_gather | solution.py:45
  261.4 2.9 gather_fusion
  264.3 1.9 convolution_bitcast_fusion
  266.1 2.0 copy.31
  268.1 0.6 convolution_convert_fusion
  268.8 1.8 convert_reduce_fusion
  270.5 1.2 fusion.11
  271.7 1.1 convolution_bitcast_fusion.1
  272.9 79.9 %all-reduce.7.cloned.1.call-done = (f32[128,1024]{0,1:T(8,128)}, f32[128,1024]{0,1:T(8,128)}) async-done(((f32[128,1024]{0,1:T(8,128)}, f32[128,1024]{0,1:T(8,128)}), (f32[128,1024]{0,1:T(8,128)}, f32[128,1024]{0,1:T(8,128)})) %all-reduce.7.cloned.1.call-update) | async-done | bytes 1048592 | tf_op jit(solution)/shard_map/psum | solution.py:11
  352.8 14.9 %psum.46 = f32[1024]{0:T(1024)S(1)} all-reduce(f32[1024]{0:T(1024)S(1)} %get-tuple-element.7), channel_id=1, replica_groups=mesh['dp'=8,'feat'=64] {'dp'}, use_global_device_ids=true, to_apply=%region_5.0 | all-reduce | flops 1024 | bytes 8192 | tf_op jit(solution)/shard_map/psum | solution.py:11
  367.7 124.8 %psum.47 = f32[1024]{0:T(1024)S(1)} all-reduce(f32[1024]{0:T(1024)S(1)} %psum.46), channel_id=1, replica_groups=mesh['dp'=8,'feat'=64] {'feat'}, use_global_device_ids=true, to_apply=%region_6.0 | all-reduce | flops 1024 | bytes 8192 | tf_op jit(solution)/shard_map/psum | solution.py:11
  492.4 0.6 dynamic_slice.11
  493.0 60.1 %all-reduce.5.cloned.1.call-done = (f32[128,1024]{0,1:T(8,128)}, f32[128,1024]{0,1:T(8,128)}) async-done(((f32[128,1024]{0,1:T(8,128)}, f32[128,1024]{0,1:T(8,128)}), (f32[128,1024]{0,1:T(8,128)}, f32[128,1024]{0,1:T(8,128)})) %all-reduce.5.cloned.1.call-update) | async-done | bytes 1048592 | tf_op jit(solution)/shard_map/psum | solution.py:11
  553.1 1.3 constant_dynamic-slice_fusion
  (26 shorter events, 0.5 us)
Async XLA Ops:
  7.2 257.1 %copy-start = (bf16[1,24,128,128]{3,2,1,0:T(8,128)(2,1)S(1)}, bf16[1,24,128,128]{3,2,1,0:T(8,128)(2,1)}, u32[]{:S(2)}) copy-start(bf16[1,24,128,128]{3,2,1,0:T(8,128)(2,1)} %param.11) | copy-start | bytes 2359300
  7.2 247.8 %all-gather.2.cloned.1.call-start = ((), (), s32[]{:S(2)}) async-start(), calls=%async_computation.1 | async-start | bytes 4259840 | tf_op jit(solution)/shard_map/all_gather | solution.py:45
  160.8 17.1 %copy-start.5 = (s32[1,24]{1,0:T(1,128)S(1)}, s32[1,24]{1,0:T(1,128)}, u32[]{:S(2)}) copy-start(s32[1,24]{1,0:T(1,128)} %param.14) | copy-start | bytes 292
  160.8 17.1 %copy-start.6 = (s32[1,24,1]{1,2,0:T(1,128)S(1)}, s32[1,24,1]{1,2,0:T(1,128)}, u32[]{:S(2)}) copy-start(s32[1,24,1]{1,2,0:T(1,128)} %param.13) | copy-start | bytes 292
  160.8 17.1 %copy-start.2 = (bf16[128,1024]{1,0:T(8,128)(2,1)S(1)}, bf16[128,1024]{1,0:T(8,128)(2,1)}, u32[]{:S(2)}) copy-start(bf16[128,1024]{1,0:T(8,128)(2,1)} %param.17) | copy-start | bytes 786436
  177.0 175.8 %all-reduce.7.cloned.1.call-start = ((), (), s32[]{:S(2)}) async-start(), calls=%async_computation.3 | async-start | bytes 2097152 | tf_op jit(solution)/shard_map/psum | solution.py:11
  261.3 6.8 %copy-start.3 = (s32[1,24]{1,0:T(1,128)S(1)}, s32[1,24]{1,0:T(1,128)}, u32[]{:S(2)}) copy-start(s32[1,24]{1,0:T(1,128)} %param.12) | copy-start | bytes 292
  264.3 4.5 copy-start.4
  268.7 3.0 copy-start.1
  272.9 280.3 %all-reduce.5.cloned.1.call-start = ((), (), s32[]{:S(2)}) async-start(), calls=%async_computation.2 | async-start | bytes 2097152 | tf_op jit(solution)/shard_map/psum | solution.py:11
Sparse Core Ops, SparseCore 0:
  177.2 77.7 all-gather.1
  273.0 79.7 all-reduce.6
  356.3 196.8 all-reduce.4
